TPU v7x, 128 devices: a whole 4x4x4 slice. The times are simulated.
128 devices in a mesh: blk: 16 (over y, x_lo, core), split: 8 (over z, x_hi).
Axes of the slice: x: 4 (x_hi: 2, x_lo: 2; x = x_hi * 2 + x_lo), y: 4, z: 4, core: 2. Of those that a mesh axis runs over, the one named last changes fastest.
Arguments:
- points: bfloat16 [65536, 128], P(('blk', 'split')), may hold values from -4 to 4
- inv_length: float32 [128], replicated, may hold values from 0.2 to 1
- amplitude: float32 [], replicated, may hold values from 0.1 to 0.4
- noise: float32 [65536], P(('blk', 'split')), may hold values from 0.1 to 1
- solution: float32 [65536, 64], P(('blk', 'split')), may hold values from -6 to 6
- residual: float32 [65536, 64], P(('blk', 'split')), may hold values from -6 to 6
- direction: float32 [65536, 64], P(('blk', 'split')), may hold values from -6 to 6
Outputs:
- solution_out: float32 [65536, 64], P(('blk', 'split'))
- residual_out: float32 [65536, 64], P(('blk', 'split'))
- direction_out: float32 [65536, 64], P(('blk', 'split'))
All inputs are finite; a program needn't handle non-finite values.
Results may differ from a plain program's by a relative error of at most 0.0045.
Values may be sent and summed in bfloat16 or wider, within the bound.
A program may use at most 64 MiB of HBM per device.

v0:
```python
import jax
import jax.numpy as jnp
from jax import lax
from jax.sharding import PartitionSpec as P


def from_behind(shard, axis, by):
    size = lax.axis_size(axis)
    return lax.ppermute(shard, axis, [(i, (i + by) % size) for i in range(size)])


def add_block(total, group_rows, group_squares, visiting, amplitude, width):
    visit_rows = visiting[:, :width]
    visit_dir = visiting[:, width:]
    visit_squares = jnp.sum(jnp.square(visit_rows.astype(jnp.float32)), axis=1)
    inner = lax.dot_general(
        group_rows, visit_rows, (((1,), (1,)), ((), ())), preferred_element_type=jnp.float32
    )
    distance = jnp.maximum(group_squares[:, None] + visit_squares[None, :] - 2.0 * inner, 0.0)
    kernel = (amplitude * jnp.exp(-0.5 * distance)).astype(jnp.bfloat16)
    return total + jnp.dot(kernel, visit_dir, preferred_element_type=jnp.float32)


def per_device(points, inv_length, amplitude, noise, solution, residual, direction):
    width = points.shape[1]
    own_count = points.shape[0]
    scaled = (points.astype(jnp.float32) * inv_length).astype(jnp.bfloat16)
    dir_half = direction.astype(jnp.bfloat16)
    group_rows = lax.all_gather(scaled, "split", axis=0, tiled=True)
    group_squares = jnp.sum(jnp.square(group_rows.astype(jnp.float32)), axis=1)
    carried = jnp.concatenate([scaled, dir_half], axis=1)
    empty = jnp.zeros((group_rows.shape[0], direction.shape[1]), jnp.float32)
    total = add_block(empty, group_rows, group_squares, carried, amplitude, width)
    cycle_size = lax.axis_size("blk")

    def advance(turn, carry):
        running, moving = carry
        moving = from_behind(moving, "blk", 1)
        return (add_block(running, group_rows, group_squares, moving, amplitude, width), moving)

    total, carried_end = lax.fori_loop(0, cycle_size - 1, advance, (total, carried))
    full_sum = lax.psum(total, "split")
    summed = lax.dynamic_slice_in_dim(full_sum, lax.axis_index("split") * own_count, own_count, 0)
    image = summed + noise[:, None] * direction
    old_norm = lax.psum(jnp.sum(residual * residual, axis=0), ("blk", "split"))
    curvature = lax.psum(jnp.sum(direction * image, axis=0), ("blk", "split"))
    step_size = old_norm / curvature
    solution_out = solution + step_size * direction
    residual_out = residual - step_size * image
    new_norm = lax.psum(jnp.sum(residual_out * residual_out, axis=0), ("blk", "split"))
    direction_out = residual_out + new_norm / old_norm * direction
    return (solution_out, residual_out, direction_out)


def solution(mesh):
    placed = (
        P(("blk", "split"), None),
        P(),
        P(),
        P(("blk", "split")),
        P(("blk", "split"), None),
        P(("blk", "split"), None),
        P(("blk", "split"), None),
    )
    return jax.shard_map(
        per_device,
        mesh=mesh,
        in_specs=placed,
        out_specs=(P(("blk", "split"), None), P(("blk", "split"), None), P(("blk", "split"), None)),
        check_vma=False,
    )
```

profile of v0, /device:TPU:1, one launch (start us, length us, event | category | flops | bytes accessed | tf_op | source)
XLA Modules:
  0.0 475.2 jit_solution(400581564594438361)
XLA Ops:
  11.5 47.8 %all-gather.2.cloned.1.call-done = bf16[4096,128]{1,0:T(8,128)(2,1)} async-done(((bf16[512,128]{1,0:T(8,128)(2,1)}), bf16[4096,128]{1,0:T(8,128)(2,1)}) %all-gather.2.cloned.1.call-update) | async-done | bytes 1048592 | tf_op jit(solution)/shard_map/all_gather | solution.py:29
  64.6 179.3 %while.12 = (s32[]{:T(128)}, f32[4096,64]{0,1:T(8,128)S(1)}, bf16[512,192]{1,0:T(8,128)(2,1)S(1)}, f32[]{:T(128)}, f32[4096]{0:T(1024)S(1)}, /*index=5*/bf16[4096,128]{1,0:T(8,128)(2,1)S(1)}, s32[]{:T(128)}) while((s32[]{:T(128)}, f32[4096,64]{0,1:T(8,128)S(1)}, bf16[512,192]{1,0:T(8,128)(2,1)S(1)}, f32[]{:T(128)}, f32[4096]{0:T(1024)S(1)}, ...), condition=%wide.region_6.0_spmd, body=%wide.region_4.6_spmd.sunk | while | flops 820444672 | bytes 4673657 | solution.py:41
  70.2 4.1 convolution_add_fusion.2
  80.4 4.1 convolution_add_fusion.2
  87.1 5.1 %collective-permute-done = bf16[512,192]{1,0:T(8,128)(2,1)S(1)} collective-permute-done((bf16[512,192]{1,0:T(8,128)(2,1)S(1)}, bf16[512,192]{1,0:T(8,128)(2,1)S(1)}, u32[]{:S(2)}, u32[]{:S(2)}) %collective-permute-start) | collective-permute-done | bytes 196640 | tf_op jit(solution)/shard_map/while/body/eval_jaxpr/ppermute | solution.py:9
  97.3 7.1 %collective-permute-done = bf16[512,192]{1,0:T(8,128)(2,1)S(1)} collective-permute-done((bf16[512,192]{1,0:T(8,128)(2,1)S(1)}, bf16[512,192]{1,0:T(8,128)(2,1)S(1)}, u32[]{:S(2)}, u32[]{:S(2)}) %collective-permute-start) | collective-permute-done | bytes 196640 | tf_op jit(solution)/shard_map/while/body/eval_jaxpr/ppermute | solution.py:9
  104.6 4.1 convolution_add_fusion.2
  108.9 7.9 %collective-permute-done = bf16[512,192]{1,0:T(8,128)(2,1)S(1)} collective-permute-done((bf16[512,192]{1,0:T(8,128)(2,1)S(1)}, bf16[512,192]{1,0:T(8,128)(2,1)S(1)}, u32[]{:S(2)}, u32[]{:S(2)}) %collective-permute-start) | collective-permute-done | bytes 196640 | tf_op jit(solution)/shard_map/while/body/eval_jaxpr/ppermute | solution.py:9
  116.9 4.1 convolution_add_fusion.2
  121.2 7.9 %collective-permute-done = bf16[512,192]{1,0:T(8,128)(2,1)S(1)} collective-permute-done((bf16[512,192]{1,0:T(8,128)(2,1)S(1)}, bf16[512,192]{1,0:T(8,128)(2,1)S(1)}, u32[]{:S(2)}, u32[]{:S(2)}) %collective-permute-start) | collective-permute-done | bytes 196640 | tf_op jit(solution)/shard_map/while/body/eval_jaxpr/ppermute | solution.py:9
  133.4 7.9 %collective-permute-done = bf16[512,192]{1,0:T(8,128)(2,1)S(1)} collective-permute-done((bf16[512,192]{1,0:T(8,128)(2,1)S(1)}, bf16[512,192]{1,0:T(8,128)(2,1)S(1)}, u32[]{:S(2)}, u32[]{:S(2)}) %collective-permute-start) | collective-permute-done | bytes 196640 | tf_op jit(solution)/shard_map/while/body/eval_jaxpr/ppermute | solution.py:9
  145.7 7.9 %collective-permute-done = bf16[512,192]{1,0:T(8,128)(2,1)S(1)} collective-permute-done((bf16[512,192]{1,0:T(8,128)(2,1)S(1)}, bf16[512,192]{1,0:T(8,128)(2,1)S(1)}, u32[]{:S(2)}, u32[]{:S(2)}) %collective-permute-start) | collective-permute-done | bytes 196640 | tf_op jit(solution)/shard_map/while/body/eval_jaxpr/ppermute | solution.py:9
  158.0 7.9 %collective-permute-done = bf16[512,192]{1,0:T(8,128)(2,1)S(1)} collective-permute-done((bf16[512,192]{1,0:T(8,128)(2,1)S(1)}, bf16[512,192]{1,0:T(8,128)(2,1)S(1)}, u32[]{:S(2)}, u32[]{:S(2)}) %collective-permute-start) | collective-permute-done | bytes 196640 | tf_op jit(solution)/shard_map/while/body/eval_jaxpr/ppermute | solution.py:9
  166.1 4.1 convolution_add_fusion.2
  170.3 7.9 %collective-permute-done = bf16[512,192]{1,0:T(8,128)(2,1)S(1)} collective-permute-done((bf16[512,192]{1,0:T(8,128)(2,1)S(1)}, bf16[512,192]{1,0:T(8,128)(2,1)S(1)}, u32[]{:S(2)}, u32[]{:S(2)}) %collective-permute-start) | collective-permute-done | bytes 196640 | tf_op jit(solution)/shard_map/while/body/eval_jaxpr/ppermute | solution.py:9
  178.4 4.1 convolution_add_fusion.2
  182.6 7.9 %collective-permute-done = bf16[512,192]{1,0:T(8,128)(2,1)S(1)} collective-permute-done((bf16[512,192]{1,0:T(8,128)(2,1)S(1)}, bf16[512,192]{1,0:T(8,128)(2,1)S(1)}, u32[]{:S(2)}, u32[]{:S(2)}) %collective-permute-start) | collective-permute-done | bytes 196640 | tf_op jit(solution)/shard_map/while/body/eval_jaxpr/ppermute | solution.py:9
  194.9 7.9 %collective-permute-done = bf16[512,192]{1,0:T(8,128)(2,1)S(1)} collective-permute-done((bf16[512,192]{1,0:T(8,128)(2,1)S(1)}, bf16[512,192]{1,0:T(8,128)(2,1)S(1)}, u32[]{:S(2)}, u32[]{:S(2)}) %collective-permute-start) | collective-permute-done | bytes 196640 | tf_op jit(solution)/shard_map/while/body/eval_jaxpr/ppermute | solution.py:9
  207.2 7.9 %collective-permute-done = bf16[512,192]{1,0:T(8,128)(2,1)S(1)} collective-permute-done((bf16[512,192]{1,0:T(8,128)(2,1)S(1)}, bf16[512,192]{1,0:T(8,128)(2,1)S(1)}, u32[]{:S(2)}, u32[]{:S(2)}) %collective-permute-start) | collective-permute-done | bytes 196640 | tf_op jit(solution)/shard_map/while/body/eval_jaxpr/ppermute | solution.py:9
  219.4 7.9 %collective-permute-done = bf16[512,192]{1,0:T(8,128)(2,1)S(1)} collective-permute-done((bf16[512,192]{1,0:T(8,128)(2,1)S(1)}, bf16[512,192]{1,0:T(8,128)(2,1)S(1)}, u32[]{:S(2)}, u32[]{:S(2)}) %collective-permute-start) | collective-permute-done | bytes 196640 | tf_op jit(solution)/shard_map/while/body/eval_jaxpr/ppermute | solution.py:9
  231.7 7.9 %collective-permute-done = bf16[512,192]{1,0:T(8,128)(2,1)S(1)} collective-permute-done((bf16[512,192]{1,0:T(8,128)(2,1)S(1)}, bf16[512,192]{1,0:T(8,128)(2,1)S(1)}, u32[]{:S(2)}, u32[]{:S(2)}) %collective-permute-start) | collective-permute-done | bytes 196640 | tf_op jit(solution)/shard_map/while/body/eval_jaxpr/ppermute | solution.py:9
  245.1 87.6 %all-reduce.3.cloned.1.call-done = f32[4096,64]{0,1:T(8,128)} async-done(((f32[4096,64]{0,1:T(8,128)}), f32[4096,64]{0,1:T(8,128)}) %all-reduce.3.cloned.1.call-update) | async-done | bytes 1048592 | tf_op jit(solution)/shard_map/psum | solution.py:42
  333.8 68.0 %all-reduce = (f32[64]{0:T(128)S(1)}, f32[64]{0:T(128)S(1)}) all-reduce(f32[64]{0:T(128)S(1)} %multiply_reduce_fusion.5, f32[64]{0:T(128)S(1)} %multiply_reduce_fusion.4), channel_id=1, replica_groups=mesh['blk'=16,'split'=8] {'blk','split'}, use_global_device_ids=true, to_apply=%region_1.0 | all-reduce | flops 128 | bytes 1024 | tf_op jit(solution)/shard_map/psum | solution.py:45
  403.5 64.1 %psum.31 = f32[64]{0:T(128)S(1)} all-reduce(f32[64]{0:T(128)S(1)} %get-tuple-element.50), channel_id=1, replica_groups=mesh['blk'=16,'split'=8] {'blk','split'}, use_global_device_ids=true, to_apply=%region_11.0 | all-reduce | flops 64 | bytes 512 | tf_op jit(solution)/shard_map/psum | solution.py:50
  (87 shorter events, 68.6 us)
Async XLA Ops:
  7.2 52.2 %all-gather.2.cloned.1.call-start = ((), (), s32[]{:S(2)}) async-start(), calls=%async_computation | async-start | bytes 1179648 | tf_op jit(solution)/shard_map/all_gather | solution.py:29
  8.8 52.5 %copy-start.1 = (bf16[512,128]{1,0:T(8,128)(2,1)S(1)}, bf16[512,128]{1,0:T(8,128)(2,1)}, u32[]{:S(2)}) copy-start(bf16[512,128]{1,0:T(8,128)(2,1)} %get-tuple-element.53) | copy-start | bytes 393220
  8.8 323.9 %all-reduce.3.cloned.1.call-start = ((), (), s32[]{:S(2)}) async-start(), calls=%async_computation.1 | async-start | bytes 2097152 | tf_op jit(solution)/shard_map/psum | solution.py:42
  59.4 1.9 copy-start.2
  64.6 5.4 %collective-permute-start = (bf16[512,192]{1,0:T(8,128)(2,1)S(1)}, bf16[512,192]{1,0:T(8,128)(2,1)S(1)}, u32[]{:S(2)}, u32[]{:S(2)}) collective-permute-start(bf16[512,192]{1,0:T(8,128)(2,1)S(1)} %get-tuple-element.101), channel_id=1, source_target_pairs={{0,8},{8,16},{16,24},{24,32},{32,40},{40,48},{48,56},{56,64},{64,7... | collective-permute-start | bytes 589832 | tf_op jit(solution)/shard_map/while/body/eval_jaxpr/ppermute | solution.py:9
  74.4 5.9 %collective-permute-start = (bf16[512,192]{1,0:T(8,128)(2,1)S(1)}, bf16[512,192]{1,0:T(8,128)(2,1)S(1)}, u32[]{:S(2)}, u32[]{:S(2)}) collective-permute-start(bf16[512,192]{1,0:T(8,128)(2,1)S(1)} %get-tuple-element.101), channel_id=1, source_target_pairs={{0,8},{8,16},{16,24},{24,32},{32,40},{40,48},{48,56},{56,64},{64,7... | collective-permute-start | bytes 589832 | tf_op jit(solution)/shard_map/while/body/eval_jaxpr/ppermute | solution.py:9
  84.6 7.6 %collective-permute-start = (bf16[512,192]{1,0:T(8,128)(2,1)S(1)}, bf16[512,192]{1,0:T(8,128)(2,1)S(1)}, u32[]{:S(2)}, u32[]{:S(2)}) collective-permute-start(bf16[512,192]{1,0:T(8,128)(2,1)S(1)} %get-tuple-element.101), channel_id=1, source_target_pairs={{0,8},{8,16},{16,24},{24,32},{32,40},{40,48},{48,56},{56,64},{64,7... | collective-permute-start | bytes 589832 | tf_op jit(solution)/shard_map/while/body/eval_jaxpr/ppermute | solution.py:9
  96.5 8.0 %collective-permute-start = (bf16[512,192]{1,0:T(8,128)(2,1)S(1)}, bf16[512,192]{1,0:T(8,128)(2,1)S(1)}, u32[]{:S(2)}, u32[]{:S(2)}) collective-permute-start(bf16[512,192]{1,0:T(8,128)(2,1)S(1)} %get-tuple-element.101), channel_id=1, source_target_pairs={{0,8},{8,16},{16,24},{24,32},{32,40},{40,48},{48,56},{56,64},{64,7... | collective-permute-start | bytes 589832 | tf_op jit(solution)/shard_map/while/body/eval_jaxpr/ppermute | solution.py:9
  108.8 8.0 %collective-permute-start = (bf16[512,192]{1,0:T(8,128)(2,1)S(1)}, bf16[512,192]{1,0:T(8,128)(2,1)S(1)}, u32[]{:S(2)}, u32[]{:S(2)}) collective-permute-start(bf16[512,192]{1,0:T(8,128)(2,1)S(1)} %get-tuple-element.101), channel_id=1, source_target_pairs={{0,8},{8,16},{16,24},{24,32},{32,40},{40,48},{48,56},{56,64},{64,7... | collective-permute-start | bytes 589832 | tf_op jit(solution)/shard_map/while/body/eval_jaxpr/ppermute | solution.py:9
  121.1 8.0 %collective-permute-start = (bf16[512,192]{1,0:T(8,128)(2,1)S(1)}, bf16[512,192]{1,0:T(8,128)(2,1)S(1)}, u32[]{:S(2)}, u32[]{:S(2)}) collective-permute-start(bf16[512,192]{1,0:T(8,128)(2,1)S(1)} %get-tuple-element.101), channel_id=1, source_target_pairs={{0,8},{8,16},{16,24},{24,32},{32,40},{40,48},{48,56},{56,64},{64,7... | collective-permute-start | bytes 589832 | tf_op jit(solution)/shard_map/while/body/eval_jaxpr/ppermute | solution.py:9
  133.4 8.0 %collective-permute-start = (bf16[512,192]{1,0:T(8,128)(2,1)S(1)}, bf16[512,192]{1,0:T(8,128)(2,1)S(1)}, u32[]{:S(2)}, u32[]{:S(2)}) collective-permute-start(bf16[512,192]{1,0:T(8,128)(2,1)S(1)} %get-tuple-element.101), channel_id=1, source_target_pairs={{0,8},{8,16},{16,24},{24,32},{32,40},{40,48},{48,56},{56,64},{64,7... | collective-permute-start | bytes 589832 | tf_op jit(solution)/shard_map/while/body/eval_jaxpr/ppermute | solution.py:9
  145.6 8.0 %collective-permute-start = (bf16[512,192]{1,0:T(8,128)(2,1)S(1)}, bf16[512,192]{1,0:T(8,128)(2,1)S(1)}, u32[]{:S(2)}, u32[]{:S(2)}) collective-permute-start(bf16[512,192]{1,0:T(8,128)(2,1)S(1)} %get-tuple-element.101), channel_id=1, source_target_pairs={{0,8},{8,16},{16,24},{24,32},{32,40},{40,48},{48,56},{56,64},{64,7... | collective-permute-start | bytes 589832 | tf_op jit(solution)/shard_map/while/body/eval_jaxpr/ppermute | solution.py:9
  157.9 8.0 %collective-permute-start = (bf16[512,192]{1,0:T(8,128)(2,1)S(1)}, bf16[512,192]{1,0:T(8,128)(2,1)S(1)}, u32[]{:S(2)}, u32[]{:S(2)}) collective-permute-start(bf16[512,192]{1,0:T(8,128)(2,1)S(1)} %get-tuple-element.101), channel_id=1, source_target_pairs={{0,8},{8,16},{16,24},{24,32},{32,40},{40,48},{48,56},{56,64},{64,7... | collective-permute-start | bytes 589832 | tf_op jit(solution)/shard_map/while/body/eval_jaxpr/ppermute | solution.py:9
  170.2 8.0 %collective-permute-start = (bf16[512,192]{1,0:T(8,128)(2,1)S(1)}, bf16[512,192]{1,0:T(8,128)(2,1)S(1)}, u32[]{:S(2)}, u32[]{:S(2)}) collective-permute-start(bf16[512,192]{1,0:T(8,128)(2,1)S(1)} %get-tuple-element.101), channel_id=1, source_target_pairs={{0,8},{8,16},{16,24},{24,32},{32,40},{40,48},{48,56},{56,64},{64,7... | collective-permute-start | bytes 589832 | tf_op jit(solution)/shard_map/while/body/eval_jaxpr/ppermute | solution.py:9
  182.5 8.0 %collective-permute-start = (bf16[512,192]{1,0:T(8,128)(2,1)S(1)}, bf16[512,192]{1,0:T(8,128)(2,1)S(1)}, u32[]{:S(2)}, u32[]{:S(2)}) collective-permute-start(bf16[512,192]{1,0:T(8,128)(2,1)S(1)} %get-tuple-element.101), channel_id=1, source_target_pairs={{0,8},{8,16},{16,24},{24,32},{32,40},{40,48},{48,56},{56,64},{64,7... | collective-permute-start | bytes 589832 | tf_op jit(solution)/shard_map/while/body/eval_jaxpr/ppermute | solution.py:9
  194.8 8.0 %collective-permute-start = (bf16[512,192]{1,0:T(8,128)(2,1)S(1)}, bf16[512,192]{1,0:T(8,128)(2,1)S(1)}, u32[]{:S(2)}, u32[]{:S(2)}) collective-permute-start(bf16[512,192]{1,0:T(8,128)(2,1)S(1)} %get-tuple-element.101), channel_id=1, source_target_pairs={{0,8},{8,16},{16,24},{24,32},{32,40},{40,48},{48,56},{56,64},{64,7... | collective-permute-start | bytes 589832 | tf_op jit(solution)/shard_map/while/body/eval_jaxpr/ppermute | solution.py:9
  207.1 8.0 %collective-permute-start = (bf16[512,192]{1,0:T(8,128)(2,1)S(1)}, bf16[512,192]{1,0:T(8,128)(2,1)S(1)}, u32[]{:S(2)}, u32[]{:S(2)}) collective-permute-start(bf16[512,192]{1,0:T(8,128)(2,1)S(1)} %get-tuple-element.101), channel_id=1, source_target_pairs={{0,8},{8,16},{16,24},{24,32},{32,40},{40,48},{48,56},{56,64},{64,7... | collective-permute-start | bytes 589832 | tf_op jit(solution)/shard_map/while/body/eval_jaxpr/ppermute | solution.py:9
  219.4 8.0 %collective-permute-start = (bf16[512,192]{1,0:T(8,128)(2,1)S(1)}, bf16[512,192]{1,0:T(8,128)(2,1)S(1)}, u32[]{:S(2)}, u32[]{:S(2)}) collective-permute-start(bf16[512,192]{1,0:T(8,128)(2,1)S(1)} %get-tuple-element.101), channel_id=1, source_target_pairs={{0,8},{8,16},{16,24},{24,32},{32,40},{40,48},{48,56},{56,64},{64,7... | collective-permute-start | bytes 589832 | tf_op jit(solution)/shard_map/while/body/eval_jaxpr/ppermute | solution.py:9
  231.7 8.0 %collective-permute-start = (bf16[512,192]{1,0:T(8,128)(2,1)S(1)}, bf16[512,192]{1,0:T(8,128)(2,1)S(1)}, u32[]{:S(2)}, u32[]{:S(2)}) collective-permute-start(bf16[512,192]{1,0:T(8,128)(2,1)S(1)} %get-tuple-element.101), channel_id=1, source_target_pairs={{0,8},{8,16},{16,24},{24,32},{32,40},{40,48},{48,56},{56,64},{64,7... | collective-permute-start | bytes 589832 | tf_op jit(solution)/shard_map/while/body/eval_jaxpr/ppermute | solution.py:9
  243.9 1.1 copy-start.4
  244.0 88.8 %copy-start = (f32[512,64]{0,1:T(8,128)S(1)}, f32[512,64]{0,1:T(8,128)}, u32[]{:S(2)}) copy-start(f32[512,64]{0,1:T(8,128)} %param.15) | copy-start | bytes 393220
  244.0 88.8 %copy-start.7 = (f32[512]{0:T(512)S(1)}, f32[512]{0:T(512)}, u32[]{:S(2)}) copy-start(f32[512]{0:T(512)} %param.12) | copy-start | bytes 6148
  244.0 157.8 %copy-start.6 = (f32[512,64]{0,1:T(8,128)S(1)}, f32[512,64]{0,1:T(8,128)}, u32[]{:S(2)}) copy-start(f32[512,64]{0,1:T(8,128)} %param.13) | copy-start | bytes 393220
  403.5 64.9 %copy-start.5 = (f32[512,64]{0,1:T(8,128)}, f32[512,64]{0,1:T(8,128)S(1)}, u32[]{:S(2)}) copy-start(f32[512,64]{0,1:T(8,128)S(1)} %get-tuple-element.51) | copy-start | bytes 393220
  (1 other events, 1.0 us)
Sparse Core Ops, SparseCore 0:
  10.9 48.4 all-gather.1
  245.1 87.5 all-reduce.2
where the time goes:
time: 476 us; the launch traced here: 475 us
  waiting for transfers between devices  241 us (51%)
  blocking collectives  132 us (28%)
  matrix products  65 us (14%)
  between operations  14.8 us (3%)
  other arithmetic  10.3 us (2%)
  starting transfers between devices  8.96 us (2%)
    ppermute x15, waiting for transfers between devices, from_behind(): lax.ppermute(shard, axis, [(i, (i + by) % size) for i in range(size)])  106 us
    psum x1, waiting for transfers between devices, per_device(): full_sum = lax.psum(total, 'split')  87.6 us
    psum x1, blocking collectives, per_device(): old_norm = lax.psum(jnp.sum(residual * residual, axis=0), ('blk', 'split'))  68 us
    dot_general x16, matrix products, add_block(): jnp.dot(kernel, visit_dir, preferred_element_type=jnp.float32)  65 us
    psum x1, blocking collectives, per_device(): lax.psum(jnp.sum(residual_out * residual_out, axis=0), ('blk', 'split'))  64.1 us
    all_gather x1, waiting for transfers between devices, per_device(): group_rows = lax.all_gather(scaled, 'split', axis=0, tiled=True)  47.8 us
  transfers between devices with their start and end apart: 17, of which 17 were waited for; matrix products, arithmetic and copies ran while one was open for 0% of the time, Pallas kernels for 0%

commit v1 on v0

v1 whole, which is shorter than its diff:
```python
import functools

import jax
import jax.numpy as jnp
from jax import lax
from jax.experimental import pallas as pl
from jax.experimental.pallas import tpu as pltpu
from jax.sharding import PartitionSpec as P

F32 = jnp.float32
BF16 = jnp.bfloat16
MESH = pl.DeviceIdType.MESH

I_SLOTS = ((0, 0), (0, 1), (1, 0), (3, 0), (2, 0), (1, 1), (3, 1), (2, 1))
J_SLOTS = (
    (0, 0), (0, 1), (0, 3), (1, 0), (3, 0), (0, 2), (2, 0), (1, 1),
    (1, 3), (3, 1), (3, 3), (1, 2), (3, 2), (2, 1), (2, 3), (2, 2),
)
N_I, N_J = len(I_SLOTS), len(J_SLOTS)
LINE_J = range(1, 7)
NEAR_J = range(1, 5)
LINE_I = range(1, 5)
ROWS = 512
FEAT = 128
COLS = 64
TILE = 256
PACK = 32
HALF = (0, TILE + PACK + 2 * COLS)
DIRS = (TILE + PACK, TILE + PACK + 2 * COLS + TILE)
SHIP = 2 * (TILE + 2 * COLS) + PACK
PIECE = ((0, HALF[1]), (HALF[1], SHIP - HALF[1]))
I_SHIP = FEAT + 16

RECTS = (
    (0, 1, 2, 0, 2, "i"),
    (2, 1, 2, 0, 2, "i"),
    (5, 1, 2, 0, 2, "i"),
    (4, 3, 2, 0, 2, "i"),
    (0, 1, 8, 2, 2, "i"),
    (2, 1, 6, 4, 2, "i"),
    (7, -1, 6, 6, 2, "p"),
    (1, -1, 2, 4, 4, "p"),
)
ORDER = [
    (i0 + s * (n % ni if fast == "i" else n // np_), p0 + (n // ni if fast == "i" else n % np_))
    for i0, s, ni, p0, np_, fast in RECTS
    for n in range(ni * np_)
]
PHASE = sum(r[2] * r[4] for r in RECTS[:-2])
UNITS = len(ORDER)
FIRST_I = [min(u for u in range(UNITS) if ORDER[u][0] == k) for k in range(N_I)]
DONE_I = [max(u for u in range(UNITS) if ORDER[u][0] == k) for k in range(N_I)]
FIRST_J = [min(u for u in range(UNITS) if ORDER[u][1] == k // 2) for k in range(N_J)]
BODY = 4
FAR = 3


def i_back(k):
    dx, dc = I_SLOTS[k]
    return I_SLOTS.index(((4 - dx) % 4, dc))


def j_back(k):
    dy, dz = J_SLOTS[k]
    return J_SLOTS.index(((4 - dy) % 4, (4 - dz) % 4))


def place():
    b = lax.axis_index("blk")
    s = lax.axis_index("split")
    return (s % 2) * 2 + (b // 2) % 2, b // 4, s // 2, b % 2


def peer(dx, dy, dz, dc):
    x, y, z, c = place()
    x, y, z, c = (x + dx) % 4, (y + dy) % 4, (z + dz) % 4, (c + dc) % 2
    return {"blk": (y * 2 + x % 2) * 2 + c, "split": z * 2 + x // 2}


def i_peer(k):
    dx, dc = I_SLOTS[k]
    return peer(dx, 0, 0, dc)


def j_peer(k):
    dy, dz = J_SLOTS[k]
    return peer(0, dy, dz, 0)


def three(v):
    hi = v.astype(BF16).astype(F32)
    mid = (v - hi).astype(BF16).astype(F32)
    return hi, mid, v - hi - mid


def marked(b, passes):
    return jnp.right_shift(sum(1 << w for w in passes), b) % 2 == 1


def where_is(u):
    ik = jp = jnp.int32(0)
    start = UNITS
    for i0, s, ni, p0, np_, fast in reversed(RECTS):
        end, start = start, start - ni * np_
        v = u - start
        i, p = (v % ni, v // ni) if fast == "i" else (v // np_, v % np_)
        ik = jnp.where(u < end, i0 + s * i, ik)
        jp = jnp.where(u < end, p0 + p, jp)
    return ik, jp


def kernel(
    points_in, inv_length_in, amplitude, noise_in, sol_in, res_in, dir_in,
    sol_out, res_out, dir_out,
    points, inv_length, noise, sol, res, dirn,
    it, jb, jsq, oacc, kbuf, sbuf, mbuf, fbuf, stat,
    in_sem, i_send, i_recv, j_send, j_recv, f_send, m_recv, r_send, r_recv, a_send, a_recv, b_send, b_recv,
):
    fetch = [
        pltpu.make_async_copy(src, dst, in_sem.at[n])
        for n, (src, dst) in enumerate(
            ((points_in, points), (inv_length_in, inv_length), (dir_in, dirn), (noise_in, noise), (res_in, res), (sol_in, sol))
        )
    ]
    for copy in fetch:
        copy.start()
    barrier = pltpu.get_barrier_semaphore()
    for k in LINE_I:
        pl.semaphore_signal(barrier, inc=1, device_id=i_peer(k), device_id_type=MESH)
    for k in LINE_J:
        pl.semaphore_signal(barrier, inc=1, device_id=j_peer(k), device_id_type=MESH)

    for copy in fetch[:3]:
        copy.wait()
    scaled = (points[...].astype(F32) * inv_length[...]).astype(BF16)
    scaled32 = scaled.astype(F32)
    log_amp = jnp.log(jnp.full((1, ROWS), amplitude[0, 0], F32))
    scaled_t = jnp.transpose(scaled32)
    it[0, pl.ds(0, FEAT), :] = scaled_t.astype(BF16)
    high = -0.5 * jnp.sum(scaled_t * scaled_t, axis=0, keepdims=True) + log_amp
    hi, mid, low = three(high)
    sub = lax.broadcasted_iota(jnp.int32, (16, ROWS), 0) % 8
    pattern = jnp.where(sub < 3, 1.0, jnp.where(sub == 3, hi, jnp.where(sub == 4, mid, jnp.where(sub == 5, low, 0.0))))
    it[0, pl.ds(FEAT, 16), :] = pattern.astype(BF16)
    half = -0.5 * jnp.sum(scaled32 * scaled32, axis=1, keepdims=True)
    hi, mid, low = three(half)
    lane = lax.broadcasted_iota(jnp.int32, (PACK, FEAT), 1)
    group, part = lane // 8, lane % 8
    packed = jnp.zeros((PACK, FEAT), F32)
    for b in range(ROWS // PACK):
        rows = slice(b * PACK, (b + 1) * PACK)
        value = jnp.where(part == 0, hi[rows], jnp.where(part == 1, mid[rows], low[rows]))
        value = jnp.where(part < 3, value, jnp.where(part < 6, 1.0, 0.0))
        packed = jnp.where(group == b, value, packed)
    jb[0, pl.ds(TILE, PACK), :] = packed.astype(BF16)
    for side in range(2):
        jb[0, pl.ds(HALF[side], TILE), :] = scaled[side * TILE : (side + 1) * TILE]
        for b in range(2):
            start = side * TILE + b * FEAT
            jb[0, pl.ds(DIRS[side] + b * COLS, COLS), :] = dirn[:, pl.ds(start, FEAT)].astype(BF16)

    def remote(src, dst, send, recv, to):
        return pltpu.make_async_remote_copy(
            src_ref=src, dst_ref=dst, send_sem=send, recv_sem=recv, device_id=to, device_id_type=MESH
        )

    def i_copy(k):
        back = i_back(k)
        return remote(it.at[0, pl.ds(0, I_SHIP)], it.at[back, pl.ds(0, I_SHIP)], i_send.at[k], i_recv.at[back], i_peer(k))

    def i_pass(k):
        return remote(
            it.at[k, pl.ds(0, I_SHIP)], it.at[k + 3, pl.ds(0, I_SHIP)], i_send.at[k + 3], i_recv.at[k + 3], i_peer(1)
        )

    def j_copy(k, piece):
        back = j_back(k)
        rows = pl.ds(*PIECE[piece])
        return remote(
            jb.at[0, rows], jb.at[back, rows], j_send.at[k, piece], j_recv.at[back, piece], j_peer(k)
        )

    def j_pass(k, n):
        dy, dz = J_SLOTS[k]
        piece = 0 if dz else 1
        to = J_SLOTS.index((n, 0) if dz else (0, n))
        lands = J_SLOTS.index((4 - n, dz) if dz else (dy, 4 - n))
        rows = pl.ds(*PIECE[piece])
        return remote(
            jb.at[k, rows], jb.at[lands, rows], f_send.at[k, n], j_recv.at[lands, piece], j_peer(to)
        )

    def j_line(k):
        dz = J_SLOTS[k][1]
        piece, lands, to = (0 if k in (1, 3) else 1), (5 if dz else 6), j_back(k)
        rows = pl.ds(*PIECE[piece])
        return remote(
            jb.at[k, rows], jb.at[lands, rows], f_send.at[k, 0], j_recv.at[lands, piece], j_peer(to)
        )

    def mix_copy(k):
        return remote(sbuf.at[k], mbuf.at[k - 3], r_send.at[k], m_recv.at[k - 3], i_peer(1))

    def r_copy(k):
        back = i_back(k)
        return remote(sbuf.at[k], fbuf.at[back], r_send.at[k], r_recv.at[back], i_peer(k))

    pl.semaphore_wait(barrier, len(LINE_I) + len(LINE_J))
    for k in LINE_I:
        i_copy(k).start()
    for piece in range(2):
        for k in NEAR_J:
            j_copy(k, piece).start()
    oacc[...] = jnp.zeros_like(oacc)

    def spread(k):
        packed = jb[k, pl.ds(TILE, PACK), :].astype(F32)
        for b in range(ROWS // PACK):
            jsq[k, pl.ds(b * PACK, PACK), :] = jnp.where(group == b, packed, 0.0).astype(BF16)

    spread(0)

    def fill(k):
        two = it[k, pl.ds(FEAT, 16), :]
        for r in range(FEAT + 16, TILE, 16):
            it[k, pl.ds(r, 16), :] = two

    fill(0)

    def want_i(k):
        if k in LINE_I:
            i_copy(i_back(k)).wait_recv()
            if k != 1:
                i_pass(k).start()
        else:
            i_pass(k - 3).wait_recv()
        fill(k)

    def want_j(k, piece):
        j_copy(j_back(k), piece).wait_recv()
        if piece == 0:
            spread(k)
        dy, dz = J_SLOTS[k]
        if k in NEAR_J and piece == (0 if k in (1, 3) else 1):
            j_line(k).start()
        if k in LINE_J and piece == (0 if dz else 1):
            for n in (1, 3):
                j_pass(k, n).start()

    def pass_far(k):
        j_pass(k, 2).start()

    events = {}

    def at(u, *what):
        events.setdefault(u, []).append(what)

    for k in range(1, N_I):
        at((FIRST_I[k] - 1) // BODY, want_i, k)
    for k in range(1, N_J):
        passed = 0 if J_SLOTS[k][1] else 1
        use = (FIRST_J[k] - 1) // BODY
        if k in LINE_J:
            at(min(use, 0 if k < 5 else FAR), want_j, k, passed)
            at(use, want_j, k, 1 - passed)
            at(1 if k in NEAR_J else FAR, pass_far, k)
        else:
            at(use, want_j, k, 0)
            at(use, want_j, k, 1)

    def give(k):
        if k > 4:
            sbuf[k] = oacc[k].astype(BF16)
            mix_copy(k).start()
            return
        if k > 1:
            mix_copy(k + 3).wait_recv()
            sbuf[k] = (oacc[k] + mbuf[k].astype(F32)).astype(BF16)
        else:
            sbuf[k] = oacc[k].astype(BF16)
        r_copy(k).start()

    def work(e00, e01, e10, e11, o00, o01, o10, o11):
        e_acc = ((e00, e01), (e10, e11))
        o_acc = ((o00, o01), (o10, o11))
        ceiling = jnp.log(jnp.full((8, TILE), amplitude[0, 0], F32))[0:1]

        def inner(ik, jp, t):
            for q in range(2):
                pltpu.matmul_push_rhs(it[ik, :, pl.ds(q * TILE, TILE)], 0, q)
            slot, side = 2 * jp + t // 2, t % 2
            rows = jb[slot, pl.ds(HALF[side], TILE), :]
            lhs = jnp.concatenate([rows, jsq[slot, pl.ds(side * TILE, TILE), :]], axis=1)
            for q in range(2):
                pltpu.matmul_acc_lhs(e_acc[q][t % 2], lhs, load_staged_rhs=0)

        def expo(t):
            for q in range(2):
                e = pltpu.matmul_pop(e_acc[q][t % 2])
                kbuf[t % 2, q] = jnp.exp(jnp.minimum(e, ceiling)).astype(BF16)

        def product(jp, t, turn):
            slot, base = 2 * jp + t // 2, DIRS[t % 2]
            lhs = jnp.concatenate([jb[slot, pl.ds(base, COLS), :], jb[slot, pl.ds(base + COLS, COLS), :]], axis=1)
            for q in range(2):
                pltpu.matmul_push_rhs(kbuf[t % 2, q], 1, q)
            for q in range(2):
                pltpu.matmul_acc_lhs(o_acc[q][turn], lhs, load_staged_rhs=1)

        def collect(ik, turn):
            for q in range(2):
                oacc[ik, :, pl.ds(q * TILE, TILE)] += pltpu.matmul_pop(o_acc[q][turn])

        for what in events.pop(-1, []):
            what[0](*what[1:])
        inner(0, 0, 0)
        inner(0, 0, 1)
        expo(0)

        @pl.loop(0, UNITS // BODY)
        def _(b):
            @pl.when(marked(b, events))
            def _():
                for when, actions in sorted(events.items()):

                    @pl.when(b == when)
                    def _(actions=actions):
                        for what in actions:
                            what[0](*what[1:])

            for n in range(BODY):
                u = b * BODY + n
                ik, jp = where_is(u)
                ik_next, jp_next = where_is(jnp.minimum(u + 1, UNITS - 1))
                inner(ik, jp, 2)
                expo(1)
                product(jp, 0, n % 2)
                inner(ik, jp, 3)
                expo(2)
                collect(where_is(jnp.maximum(u - 1, 0))[0], 1 - n % 2)
                product(jp, 1, n % 2)
                inner(ik_next, jp_next, 0)
                expo(3)
                product(jp, 2, n % 2)
                inner(ik_next, jp_next, 1)
                expo(0)
                product(jp, 3, n % 2)

            @pl.when(b >= PHASE // BODY)
            def _():
                collect(where_is(b * BODY + BODY - 1)[0], (BODY - 1) % 2)
                for k in range(N_I - 1, 0, -1):
                    pl.when(b == DONE_I[k] // BODY)(functools.partial(give, k))

        for q in range(2):
            spare = pltpu.matmul_pop(e_acc[q][1])
            stat[1, 0] = spare[0:8, 0:FEAT]

    pl.run_scoped(
        work,
        *[pltpu.ACC(q)((TILE, TILE), F32) for q in (0, 0, 1, 1)],
        *[pltpu.ACC(q)((COLS, TILE), F32) for q in (0, 0, 1, 1)],
    )

    for copy in fetch[3:]:
        copy.wait()
    d = dirn[...]
    r = res[...]
    image = noise[...] * d + oacc[0]
    for k in LINE_I:
        r_copy(i_back(k)).wait_recv()
        image = image + fbuf[k].astype(F32)
    lane = lax.broadcasted_iota(jnp.int32, (COLS, FEAT), 1)
    sums = jnp.zeros((COLS, FEAT), F32)
    for n, v in enumerate((r * r, d * image, r * image, image * image)):
        sums = jnp.where(lane == n, jnp.sum(v, axis=1, keepdims=True), sums)
    sums = jnp.transpose(jnp.concatenate([sums, jnp.zeros((FEAT - COLS, FEAT), F32)], axis=0))
    stat[0, 0] = sums[0:8]

    def a_copy(k):
        back = j_back(k)
        return remote(stat.at[0, 0], stat.at[0, back], a_send.at[k], a_recv.at[back], j_peer(k))

    def b_copy(k):
        back = i_back(k)
        return remote(stat.at[1, 0], stat.at[1, back], b_send.at[k], b_recv.at[back], i_peer(k))

    for k in range(1, N_J):
        a_copy(k).start()
    for k in range(1, N_J):
        a_copy(j_back(k)).wait_recv()
    stat[1, 0] = jnp.sum(stat[0], axis=0)
    for k in range(1, N_I):
        b_copy(k).start()
    for k in range(1, N_I):
        b_copy(i_back(k)).wait_recv()
    total = jnp.sum(stat[1, pl.ds(0, N_I)], axis=0)
    total = jnp.transpose(jnp.concatenate([total, jnp.zeros((FEAT - 8, FEAT), F32)], axis=0))
    old_norm, curvature, cross, square = [total[:COLS, n : n + 1] for n in range(4)]
    step = old_norm / curvature
    new_norm = jnp.maximum(old_norm - 2.0 * step * cross + step * step * square, 0.0)
    r_new = r - step * image
    sol_out[...] = sol[...] + step * d
    res_out[...] = r_new
    dir_out[...] = r_new + (new_norm / old_norm) * d

    for k in LINE_I:
        i_copy(k).wait_send()
    for k in (2, 3, 4):
        i_pass(k).wait_send()
    for k in LINE_J:
        if k in NEAR_J:
            for piece in range(2):
                j_copy(k, piece).wait_send()
            j_line(k).wait_send()
        for n in (1, 3, 2):
            j_pass(k, n).wait_send()
    for k in range(1, N_I):
        (mix_copy if k > 4 else r_copy)(k).wait_send()
        b_copy(k).wait_send()
    for k in range(1, N_J):
        a_copy(k).wait_send()


def per_device(points, inv_length, amplitude, noise, sol, res, dirn):
    vmem = pl.BlockSpec(memory_space=pltpu.VMEM)
    hbm = pl.BlockSpec(memory_space=pltpu.HBM)
    out = jax.ShapeDtypeStruct((COLS, ROWS), F32)
    dma = pltpu.SemaphoreType.DMA
    outs = pl.pallas_call(
        kernel,
        out_shape=(out, out, out),
        in_specs=[hbm, hbm, pl.BlockSpec(memory_space=pltpu.SMEM), hbm, hbm, hbm, hbm],
        out_specs=(vmem, vmem, vmem),
        scratch_shapes=[
            pltpu.VMEM((ROWS, FEAT), BF16),
            pltpu.VMEM((1, FEAT), F32),
            pltpu.VMEM((1, ROWS), F32),
            pltpu.VMEM((COLS, ROWS), F32),
            pltpu.VMEM((COLS, ROWS), F32),
            pltpu.VMEM((COLS, ROWS), F32),
            pltpu.VMEM((N_I, TILE, ROWS), BF16),
            pltpu.VMEM((N_J, SHIP, FEAT), BF16),
            pltpu.VMEM((N_J, ROWS, FEAT), BF16),
            pltpu.VMEM((N_I, COLS, ROWS), F32),
            pltpu.VMEM((2, 2, TILE, TILE), BF16),
            pltpu.VMEM((N_I, COLS, ROWS), BF16),
            pltpu.VMEM((5, COLS, ROWS), BF16),
            pltpu.VMEM((5, COLS, ROWS), BF16),
            pltpu.VMEM((2, N_J, 8, FEAT), F32),
            dma((6,)),
            dma((N_I,)),
            dma((N_I,)),
            dma((N_J, 2)),
            dma((N_J, 2)),
            dma((7, 4)),
            dma((5,)),
            dma((N_I,)),
            dma((5,)),
            dma((N_J,)),
            dma((N_J,)),
            dma((N_I,)),
            dma((N_I,)),
        ],
        compiler_params=pltpu.CompilerParams(
            collective_id=0, has_side_effects=True, vmem_limit_bytes=64 * 1024 * 1024
        ),
        name="cg_step",
    )(points, inv_length.reshape(1, -1), amplitude.reshape(1, 1), noise.reshape(1, -1), sol.T, res.T, dirn.T)
    return tuple(v.T for v in outs)


def solution(mesh):
    placed = (
        P(("blk", "split"), None),
        P(),
        P(),
        P(("blk", "split")),
        P(("blk", "split"), None),
        P(("blk", "split"), None),
        P(("blk", "split"), None),
    )

    def whole(*args):
        with jax.sharding.use_abstract_mesh(mesh.abstract_mesh):
            return jax.shard_map(
                per_device,
                mesh=mesh,
                in_specs=placed,
                out_specs=(P(("blk", "split"), None),) * 3,
                check_vma=False,
            )(*args)

    return whole
```

time: 476 us -> 60.5 us (0.13)
  waiting for transfers between devices: 241 us -> 0 us
  blocking collectives: 132 us -> 0 us
  matrix products: 65 us -> 0 us
  Pallas kernels: 0 us -> 55.9 us
  between operations: 14.8 us -> 1.3 us
  other arithmetic: 10.3 us -> 0 us
  starting transfers between devices: 8.96 us -> 0 us
    psum x2 -> x0, blocking collectives: 132 us -> none  [the longest x1 68 us: per_device(): old_norm = lax.psum(jnp.sum(residual * residual, axis=0), ('blk', 'split'))]
    ppermute x15 -> x0, waiting for transfers between devices: 106 us -> none  [from_behind(): lax.ppermute(shard, axis, [(i, (i + by) % size) for i in range(size)])]
    psum x1 -> x0, waiting for transfers between devices: 87.6 us -> none  [per_device(): full_sum = lax.psum(total, 'split')]
    dot_general x16 -> x0, matrix products: 65 us -> none  [add_block(): jnp.dot(kernel, visit_dir, preferred_element_type=jnp.float32)]
    pallas_call x0 -> x1, Pallas kernels: none -> 55.9 us  [per_device(): pl.pallas_call(kernel, out_shape=(out, out, out), in_specs=[hbm, hbm, pl....]
    all_gather x1 -> x0, waiting for transfers between devices: 47.8 us -> none  [per_device(): group_rows = lax.all_gather(scaled, 'split', axis=0, tiled=True)]
    ppermute x15 -> x0, starting transfers between devices: 8.88 us -> none  [from_behind(): lax.ppermute(shard, axis, [(i, (i + by) % size) for i in range(size)])]
    reduce_sum x20 -> x0, other arithmetic: 8.61 us -> none  [the longest x16 3.8 us: add_block(): visit_squares = jnp.sum(jnp.square(visit_rows.astype(jnp.float32)), axis=1)]
  transfers between devices with their start and end apart: 17 -> 0, of which waited for: 17 -> 0; matrix products, arithmetic and copies ran while one was open for 0% -> 0% of each run, Pallas kernels for 0% -> 0%
where the time goes in v1:
time: 60.5 us; the launch traced here: 60.4 us
  Pallas kernels  55.9 us (92%)
  local copies, waits for them, and re-layouts  3.21 us (5%)
  between operations  1.3 us (2%)
    pallas_call x1, Pallas kernels, per_device(): pl.pallas_call(kernel, out_shape=(out, out, out), in_specs=[hbm, hbm, pl....  55.9 us
    unnamed x7, local copies, waits for them, and re-layouts  3.21 us

profile of v1, /device:TPU:1, one launch (start us, length us, event | category | flops | bytes accessed | tf_op | source)
XLA Modules:
  0.0 60.4 jit_solution(4612711102509393484)
XLA Ops:
  1.3 55.9 %cg_step.1 = (f32[64,512]{1,0:T(8,128)}, f32[64,512]{1,0:T(8,128)}, f32[64,512]{1,0:T(8,128)}) custom-call(bf16[512,128]{1,0:T(8,128)(2,1)} %points_in.1, f32[1,128]{1,0:T(1,128)} %bitcast.17, f32[1,1]{1,0:T(1,128)} %bitcast.9.amplitude, f32[1,512]{1,0:T(1,128)} %bitcast.16, f32[64,512]{1,0:T(8,128)} %bitcast.13, f32[64,512]{1,0:T(8,128)} %bitcast.14, ...), custom_call_target="tpu_custom_call" | custom-call | tf_op jit(solution)/shard_map/cg_step/pallas_call | solution.py:430
  57.1 0.0 copy-start.1
  57.2 1.6 %copy.14 = f32[512,64]{0,1:T(8,128)} copy(f32[512,64]{0,1:T(8,128)} %bitcast.12) | data formatting | bytes 262144
  58.8 0.0 copy-done.1
  58.8 0.0 copy-start
  58.8 0.7 %copy.15 = f32[512,64]{0,1:T(8,128)} copy(f32[512,64]{0,1:T(8,128)S(1)} %bitcast.11) | data formatting | bytes 262144
  59.4 0.3 copy-done
  59.7 0.7 %copy.16 = f32[512,64]{0,1:T(8,128)} copy(f32[512,64]{0,1:T(8,128)S(1)} %bitcast.10) | data formatting | bytes 262144
Async XLA Ops:
  57.1 1.6 %copy-start.1 = (f32[64,512]{1,0:T(8,128)S(1)}, f32[64,512]{1,0:T(8,128)}, u32[]{:S(2)}) copy-start(f32[64,512]{1,0:T(8,128)} %get-tuple-element.7) | copy-start | bytes 393220
  58.8 1.0 %copy-start = (f32[64,512]{1,0:T(8,128)S(1)}, f32[64,512]{1,0:T(8,128)}, u32[]{:S(2)}) copy-start(f32[64,512]{1,0:T(8,128)} %get-tuple-element.8) | copy-start | bytes 393220

commit v2 on v1

--- a/solution.py
+++ b/solution.py
@@ -111,7 +111,7 @@
 
 def kernel(
     points_in, inv_length_in, amplitude, noise_in, sol_in, res_in, dir_in,
-    sol_out, res_out, dir_out,
+    out,
     points, inv_length, noise, sol, res, dirn,
     it, jb, jsq, oacc, kbuf, sbuf, mbuf, fbuf, stat,
     in_sem, i_send, i_recv, j_send, j_recv, f_send, m_recv, r_send, r_recv, a_send, a_recv, b_send, b_recv,
@@ -206,11 +206,14 @@
         return remote(sbuf.at[k], fbuf.at[back], r_send.at[k], r_recv.at[back], i_peer(k))
 
     pl.semaphore_wait(barrier, len(LINE_I) + len(LINE_J))
-    for k in LINE_I:
+    for k in NEAR_J:
+        j_copy(k, 0).start()
+    for k in LINE_I[:3]:
         i_copy(k).start()
-    for piece in range(2):
-        for k in NEAR_J:
-            j_copy(k, piece).start()
+    for k in NEAR_J:
+        j_copy(k, 1).start()
+    for k in LINE_I[3:]:
+        i_copy(k).start()
     oacc[...] = jnp.zeros_like(oacc)
 
     def spread(k):
@@ -263,7 +266,7 @@
         if k in LINE_J:
             at(min(use, 0 if k < 5 else FAR), want_j, k, passed)
             at(use, want_j, k, 1 - passed)
-            at(1 if k in NEAR_J else FAR, pass_far, k)
+            at(3 if k in NEAR_J else FAR + 2, pass_far, k)
         else:
             at(use, want_j, k, 0)
             at(use, want_j, k, 1)
@@ -387,23 +390,6 @@
 
     for k in range(1, N_J):
         a_copy(k).start()
-    for k in range(1, N_J):
-        a_copy(j_back(k)).wait_recv()
-    stat[1, 0] = jnp.sum(stat[0], axis=0)
-    for k in range(1, N_I):
-        b_copy(k).start()
-    for k in range(1, N_I):
-        b_copy(i_back(k)).wait_recv()
-    total = jnp.sum(stat[1, pl.ds(0, N_I)], axis=0)
-    total = jnp.transpose(jnp.concatenate([total, jnp.zeros((FEAT - 8, FEAT), F32)], axis=0))
-    old_norm, curvature, cross, square = [total[:COLS, n : n + 1] for n in range(4)]
-    step = old_norm / curvature
-    new_norm = jnp.maximum(old_norm - 2.0 * step * cross + step * step * square, 0.0)
-    r_new = r - step * image
-    sol_out[...] = sol[...] + step * d
-    res_out[...] = r_new
-    dir_out[...] = r_new + (new_norm / old_norm) * d
-
     for k in LINE_I:
         i_copy(k).wait_send()
     for k in (2, 3, 4):
@@ -417,21 +403,39 @@
             j_pass(k, n).wait_send()
     for k in range(1, N_I):
         (mix_copy if k > 4 else r_copy)(k).wait_send()
-        b_copy(k).wait_send()
+    for k in range(1, N_J):
+        a_copy(j_back(k)).wait_recv()
+    stat[1, 0] = jnp.sum(stat[0], axis=0)
+    for k in range(1, N_I):
+        b_copy(k).start()
     for k in range(1, N_J):
         a_copy(k).wait_send()
+    for k in range(1, N_I):
+        b_copy(i_back(k)).wait_recv()
+    total = jnp.sum(stat[1, pl.ds(0, N_I)], axis=0)
+    total = jnp.transpose(jnp.concatenate([total, jnp.zeros((FEAT - 8, FEAT), F32)], axis=0))
+    old_norm, curvature, cross, square = [total[:COLS, n : n + 1] for n in range(4)]
+    step = old_norm / curvature
+    new_norm = jnp.maximum(old_norm - 2.0 * step * cross + step * step * square, 0.0)
+    r_new = r - step * image
+    out[0] = sol[...] + step * d
+    out[1] = r_new
+    out[2] = r_new + (new_norm / old_norm) * d
+
+    for k in range(1, N_I):
+        b_copy(k).wait_send()
 
 
 def per_device(points, inv_length, amplitude, noise, sol, res, dirn):
     vmem = pl.BlockSpec(memory_space=pltpu.VMEM)
     hbm = pl.BlockSpec(memory_space=pltpu.HBM)
-    out = jax.ShapeDtypeStruct((COLS, ROWS), F32)
+    out = jax.ShapeDtypeStruct((3, COLS, ROWS), F32)
     dma = pltpu.SemaphoreType.DMA
     outs = pl.pallas_call(
         kernel,
-        out_shape=(out, out, out),
+        out_shape=out,
         in_specs=[hbm, hbm, pl.BlockSpec(memory_space=pltpu.SMEM), hbm, hbm, hbm, hbm],
-        out_specs=(vmem, vmem, vmem),
+        out_specs=vmem,
         scratch_shapes=[
             pltpu.VMEM((ROWS, FEAT), BF16),
             pltpu.VMEM((1, FEAT), F32),
@@ -467,7 +471,7 @@
         ),
         name="cg_step",
     )(points, inv_length.reshape(1, -1), amplitude.reshape(1, 1), noise.reshape(1, -1), sol.T, res.T, dirn.T)
-    return tuple(v.T for v in outs)
+    return outs[0].T, outs[1].T, outs[2].T
 
 
 def solution(mesh):

time: 60.5 us -> 57.9 us (0.957)
  local copies, waits for them, and re-layouts: 3.21 us -> 1.78 us
  Pallas kernels: 55.9 us -> 54.6 us
    unnamed x7 -> x0, local copies, waits for them, and re-layouts: 3.21 us -> none
    transpose x0 -> x1, local copies, waits for them, and re-layouts: none -> 1.78 us  [per_device(): return (outs[0].T, outs[1].T, outs[2].T)]
    pallas_call x1, Pallas kernels: 55.9 us -> 54.6 us  [per_device(): pl.pallas_call(kernel, out_shape=out, in_specs=[hbm, hbm, pl.BlockSpec(me...]
where the time goes in v2:
time: 57.9 us; the launch traced here: 57.7 us
  Pallas kernels  54.6 us (94%)
  local copies, waits for them, and re-layouts  1.78 us (3%)
  between operations  1.29 us (2%)
    pallas_call x1, Pallas kernels, per_device(): pl.pallas_call(kernel, out_shape=out, in_specs=[hbm, hbm, pl.BlockSpec(me...  54.6 us
    transpose x1, local copies, waits for them, and re-layouts, per_device(): return (outs[0].T, outs[1].T, outs[2].T)  1.78 us

profile of v2, /device:TPU:1, one launch (start us, length us, event | category | flops | bytes accessed | tf_op | source)
XLA Modules:
  0.0 57.7 jit_solution(13289841676615188814)
XLA Ops:
  1.3 54.6 %cg_step.1 = f32[3,64,512]{2,1,0:T(8,128)} custom-call(bf16[512,128]{1,0:T(8,128)(2,1)} %points_in.1, f32[1,128]{1,0:T(1,128)} %bitcast.23, f32[1,1]{1,0:T(1,128)} %bitcast.18.amplitude, f32[1,512]{1,0:T(1,128)} %bitcast.22, f32[64,512]{1,0:T(8,128)} %bitcast.19, f32[64,512]{1,0:T(8,128)} %bitcast.20, f32[64,512]{1,0:T(8,128)} %bitcast.21), custom_call_target="tpu_custom_call" | custom-call | tf_op jit(solution)/shard_map/cg_step/pallas_call | solution.py:434
  55.9 1.8 %slice_bitcast_fusion = (f32[512,64]{0,1:T(8,128)}, f32[512,64]{0,1:T(8,128)}, f32[512,64]{0,1:T(8,128)}) fusion(f32[3,64,512]{2,1,0:T(8,128)} %cg_step.1), kind=kLoop, calls=%fused_computation | loop fusion | bytes 786432 | tf_op jit(solution)/shard_map/transpose | solution.py:474

commit v3 on v2

--- a/solution.py
+++ b/solution.py
@@ -370,12 +370,14 @@
     d = dirn[...]
     r = res[...]
     image = noise[...] * d + oacc[0]
+    own = jnp.sum(r * r, axis=1, keepdims=True)
     for k in LINE_I:
         r_copy(i_back(k)).wait_recv()
         image = image + fbuf[k].astype(F32)
     lane = lax.broadcasted_iota(jnp.int32, (COLS, FEAT), 1)
     sums = jnp.zeros((COLS, FEAT), F32)
-    for n, v in enumerate((r * r, d * image, r * image, image * image)):
+    sums = jnp.where(lane == 0, own, sums)
+    for n, v in enumerate((d * image, r * image, image * image), 1):
         sums = jnp.where(lane == n, jnp.sum(v, axis=1, keepdims=True), sums)
     sums = jnp.transpose(jnp.concatenate([sums, jnp.zeros((FEAT - COLS, FEAT), F32)], axis=0))
     stat[0, 0] = sums[0:8]

time: 57.9 us -> 57.9 us (level)
  no operation moved by 1% of the time
where the time goes in v3:
time: 57.9 us; the launch traced here: 57.7 us
  Pallas kernels  54.7 us (94%)
  local copies, waits for them, and re-layouts  1.78 us (3%)
  between operations  1.29 us (2%)
    pallas_call x1, Pallas kernels, per_device(): pl.pallas_call(kernel, out_shape=out, in_specs=[hbm, hbm, pl.BlockSpec(me...  54.7 us
    transpose x1, local copies, waits for them, and re-layouts, per_device(): return (outs[0].T, outs[1].T, outs[2].T)  1.78 us

profile of v3, /device:TPU:1, one launch (start us, length us, event | category | flops | bytes accessed | tf_op | source)
XLA Modules:
  0.0 57.7 jit_solution(11076348027978920340)
XLA Ops:
  1.3 54.7 %cg_step.1 = f32[3,64,512]{2,1,0:T(8,128)} custom-call(bf16[512,128]{1,0:T(8,128)(2,1)} %points_in.1, f32[1,128]{1,0:T(1,128)} %bitcast.23, f32[1,1]{1,0:T(1,128)} %bitcast.18.amplitude, f32[1,512]{1,0:T(1,128)} %bitcast.22, f32[64,512]{1,0:T(8,128)} %bitcast.19, f32[64,512]{1,0:T(8,128)} %bitcast.20, f32[64,512]{1,0:T(8,128)} %bitcast.21), custom_call_target="tpu_custom_call" | custom-call | tf_op jit(solution)/shard_map/cg_step/pallas_call | solution.py:436
  56.0 1.8 %slice_bitcast_fusion = (f32[512,64]{0,1:T(8,128)}, f32[512,64]{0,1:T(8,128)}, f32[512,64]{0,1:T(8,128)}) fusion(f32[3,64,512]{2,1,0:T(8,128)} %cg_step.1), kind=kLoop, calls=%fused_computation | loop fusion | bytes 786432 | tf_op jit(solution)/shard_map/transpose | solution.py:476
